TPU v7x, 256 devices: a whole 4x4x8 slice. The times are simulated.
256 devices in a mesh: mp: 16 (over y, z_lo), fsdp: 16 (over z_hi, x, core).
Axes of the slice: x: 4, y: 4, z: 8 (z_hi: 2, z_lo: 4; z = z_hi * 4 + z_lo), core: 2. Of those that a mesh axis runs over, the one named last changes fastest.
Arguments:
- hidden: bfloat16 [16, 256, 16, 2048], P('mp', 'fsdp'), may hold values from -6 to 6
- gain: float32 [16, 2048], P('mp'), may hold values from 0.25 to 1.75
- head: bfloat16 [16, 2048, 36864], P('mp', None, 'fsdp'), may hold values from -0.125 to 0.125
- partner: int32 [16], replicated, may hold values from 0 to 15, as said below
- codes: int32 [256, 16], replicated, may hold values from 0 to 36863
Outputs:
- grad_hidden: bfloat16 [16, 256, 16, 2048], P('mp', 'fsdp')
- note_loss: float32 [16, 256], P('mp', 'fsdp')
- grad_gain: float32 [16, 2048], P('mp')
Inputs may be any that keep to these rules, and one draw needn't show every extreme that they name: partner[partner[m]] == m and partner[m] != m for every model m. `codes`: a note may list a label number more than once.
All inputs are finite; a program needn't handle non-finite values.
Results may differ from a plain program's by a relative error of at most 0.0051.
Values may be sent and summed in bfloat16 or wider, within the bound.
A program may use at most 128 MiB of HBM per device.

v0:
```python
import math

import jax
import jax.numpy as jnp
from jax import lax
from jax.sharding import PartitionSpec as P

epsilon = 1e-05
smoothing_heat_scale = 2.0
mentor_penalty_factor = 0.5


def on_device(hidden, gain, head, partner, codes):
    states = hidden[0].astype(jnp.float32)
    gains = gain[0]
    weights = head[0]
    pool_scale = 1.0 / math.sqrt(states.shape[1])
    inverse_rms = lax.rsqrt(jnp.mean(states * states, axis=-1, keepdims=True) + epsilon)
    normed = states * inverse_rms
    pooled = (jnp.sum(normed, axis=1) * gains * pool_scale).astype(jnp.bfloat16)
    learner_score_matrix = jnp.dot(
        lax.all_gather(pooled, "fsdp", axis=0, tiled=True),
        weights,
        preferred_element_type=jnp.float32,
    ).astype(jnp.bfloat16)
    models = lax.axis_size("mp")
    note_count = learner_score_matrix.shape[0]
    labels = weights.shape[1]
    all_logits = lax.all_gather(learner_score_matrix, "mp", axis=0, tiled=True).reshape(
        models, note_count, labels
    )
    peer_score_matrix = lax.dynamic_index_in_dim(
        all_logits, partner[lax.axis_index("mp")], 0, keepdims=False
    )
    label_ids = lax.axis_index("fsdp") * labels + jnp.arange(labels, dtype=jnp.int32)
    diagnosis_truth = jnp.any(codes[:, :, None] == label_ids[None, None, :], axis=1).astype(
        jnp.float32
    )
    learner_hidden_matrix = learner_score_matrix.astype(jnp.float32)
    smoothed_diagnosis_truth = jax.nn.sigmoid(
        peer_score_matrix.astype(jnp.float32) / smoothing_heat_scale
    )
    combined_cost_sum = (
        jax.nn.softplus(learner_hidden_matrix)
        - diagnosis_truth * learner_hidden_matrix
        + mentor_penalty_factor
        * smoothing_heat_scale
        * smoothing_heat_scale
        * (
            jax.nn.softplus(learner_hidden_matrix / smoothing_heat_scale)
            - smoothed_diagnosis_truth * learner_hidden_matrix / smoothing_heat_scale
        )
    )
    totals = lax.psum_scatter(
        jnp.sum(combined_cost_sum, axis=1), "fsdp", scatter_dimension=0, tiled=True
    )
    note_loss = totals / (labels * lax.axis_size("fsdp"))
    score_derivative = (
        jax.nn.sigmoid(learner_hidden_matrix)
        - diagnosis_truth
        + mentor_penalty_factor
        * smoothing_heat_scale
        * (jax.nn.sigmoid(learner_hidden_matrix / smoothing_heat_scale) - smoothed_diagnosis_truth)
    ).astype(jnp.bfloat16)
    dpooled = lax.psum_scatter(
        lax.dot_general(
            score_derivative, weights, (((1,), (1,)), ((), ())), preferred_element_type=jnp.float32
        ),
        "fsdp",
        scatter_dimension=0,
        tiled=True,
    )
    scaled_grad = dpooled * pool_scale
    gain_partial = jnp.sum(scaled_grad * jnp.sum(normed, axis=1), axis=0)
    grad_gain = lax.psum(gain_partial, "fsdp")
    dnorm = (scaled_grad * gains)[:, None, :]
    grad_hidden = inverse_rms * (dnorm - normed * jnp.mean(dnorm * normed, axis=-1, keepdims=True))
    return (grad_hidden.astype(jnp.bfloat16)[None], note_loss[None], grad_gain[None])


def solution(mesh):
    return jax.shard_map(
        on_device,
        mesh=mesh,
        in_specs=(P("mp", "fsdp", None, None), P("mp", None), P("mp", None, "fsdp"), P(), P()),
        out_specs=(P("mp", "fsdp", None, None), P("mp", "fsdp"), P("mp", None)),
        check_vma=False,
    )
```

profile of v0, /device:TPU:1, one launch (start us, length us, event | category | flops | bytes accessed | tf_op | source)
XLA Modules:
  0.0 623.1 jit_solution(9721961442733692775)
XLA Ops:
  7.2 0.0 all-gather.3.cloned.1.call-start
  7.2 1.5 fusion.39
  8.7 1.8 fusion.13
  10.5 1.3 multiply_convert_fusion
  11.9 0.0 all-gather.3.cloned.1.call-update
  11.9 0.0 all-gather.5.cloned.1.call-start
  12.0 60.0 %all-gather.3.cloned.1.call-done = bf16[256,2048]{1,0:T(8,128)(2,1)} async-done(((bf16[16,2048]{1,0:T(8,128)(2,1)}), bf16[256,2048]{1,0:T(8,128)(2,1)}) %all-gather.3.cloned.1.call-update) | async-done | bytes 1048592 | tf_op jit(solution)/shard_map/all_gather | solution.py:22
  71.9 7.6 %fusion.4 = bf16[256,2304]{1,0:T(8,128)(2,1)} fusion(bf16[256,2048]{1,0:T(8,128)(2,1)} %all-gather.3.cloned.1.call-done, bf16[1,2048,2304]{2,1,0:T(8,128)(2,1)} %param.7), kind=kOutput, calls=%fused_computation.13 | convolution fusion | flops 2416508928 | bytes 11665408 | tf_op jit(solution)/shard_map/dot_general | solution.py:21
  79.6 0.0 all-gather.5.cloned.1.call-update
  79.6 0.2 reduce-scatter.2.cloned.1.call-start
  79.8 0.6 dynamic_slice.7
  81.7 0.1 copy.10
  82.5 7.6 %compare_reduce_fusion = pred[256,2304]{1,0:T(8,128)(4,1)S(1)} fusion(s32[2304]{0:T(1024)S(1)} %iota_add_fusion, s32[256,16]{1,0:T(8,128)S(1)} %copy.10), kind=kLoop, calls=%fused_computation | loop fusion | flops 18284544 | bytes 615424 | tf_op jit(solution)/shard_map/reduce_or | solution.py:36
  90.1 381.7 %all-gather.5.cloned.1.call-done = bf16[4096,2304]{1,0:T(8,128)(2,1)} async-done(((bf16[256,2304]{1,0:T(8,128)(2,1)}), bf16[4096,2304]{1,0:T(8,128)(2,1)}) %all-gather.5.cloned.1.call-update) | async-done | bytes 18874384 | tf_op jit(solution)/shard_map/all_gather | solution.py:29
  471.8 9.6 %fusion = f32[256,2048]{1,0:T(8,128)} fusion(bf16[1,2048,2304]{2,1,0:T(8,128)(2,1)} %param.7, pred[256,2304]{1,0:T(8,128)(4,1)S(1)} %compare_reduce_fusion, bf16[256,2304]{1,0:T(8,128)(2,1)} %fusion.4, bf16[16,256,2304]{2,1,0:T(8,128)(2,1)} %bitcast.38, s32[]{:T(128)S(6)} %select_n.15), kind=kOutput, calls=%fused_computation.1 | convolution fusion | flops 2426535936 | bytes 14483460 | tf_op jit(solution)/shard_map/dot_general | solution.py:66
  481.4 0.0 reduce-scatter.2.cloned.1.call-update
  481.5 0.6 dynamic-slice
  482.7 5.3 fusion.31
  488.1 79.3 %reduce-scatter.2.cloned.1.call-done = f32[16,2048]{1,0:T(8,128)} async-done(((f32[256,2048]{1,0:T(8,128)}), f32[16,2048]{1,0:T(8,128)}) %reduce-scatter.2.cloned.1.call-update) | async-done | bytes 131088 | tf_op jit(solution)/shard_map/reduce_scatter | solution.py:65
  567.4 1.0 multiply_reduce_fusion
  568.4 0.4 fusion.38
  568.8 1.5 fusion.43
  570.2 45.8 %all-reduce.1 = (f32[256]{0:T(256)S(1)}, f32[1,2048]{1,0:T(1,128)}) all-reduce(f32[256]{0:T(256)S(1)} %fusion.31, f32[1,2048]{1,0:T(1,128)S(1)} %bitcast.37), channel_id=3, replica_groups=mesh['mp'=16,'fsdp'=16] {'fsdp'}, use_global_device_ids=true, to_apply=%region_6.7.clone | all-reduce | flops 2304 | bytes 18432
  616.0 0.6 fusion.47
  (16 shorter events, 0.1 us)
Async XLA Ops:
  7.2 64.8 %all-gather.3.cloned.1.call-start = ((), (), s32[]{:S(2)}) async-start(), calls=%async_computation.1 | async-start | bytes 1114112 | tf_op jit(solution)/shard_map/all_gather | solution.py:22
  11.9 67.9 %copy-start.4 = (s32[16]{0:T(128)S(1)}, s32[16]{0:T(128)}, u32[]{:S(2)}) copy-start(s32[16]{0:T(128)} %param.8) | copy-start | bytes 196
  11.9 69.8 %copy-start.3 = (s32[256,16]{0,1:T(8,128)S(1)}, s32[256,16]{0,1:T(8,128)}, u32[]{:S(2)}) copy-start(s32[256,16]{0,1:T(8,128)} %param.9) | copy-start | bytes 49156
  11.9 459.9 %all-gather.5.cloned.1.call-start = ((), (), s32[]{:S(2)}) async-start(), calls=%async_computation.2 | async-start | bytes 20054016 | tf_op jit(solution)/shard_map/all_gather | solution.py:29
  79.6 487.8 %reduce-scatter.2.cloned.1.call-start = ((), (), s32[]{:S(2)}) async-start(), calls=%async_computation.3 | async-start | bytes 2228224 | tf_op jit(solution)/shard_map/reduce_scatter | solution.py:65
  471.8 9.7 %copy-start.5 = (u32[256]{0:T(256)S(1)}, u32[256]{0:T(256)}, u32[]{:S(2)}) copy-start(u32[256]{0:T(256)} %constant.49) | copy-start | bytes 3076
  471.8 10.9 %copy-start.2 = (f32[1,2048]{1,0:T(1,128)S(1)}, f32[1,2048]{1,0:T(1,128)}, u32[]{:S(2)}) copy-start(f32[1,2048]{1,0:T(1,128)} %param.6) | copy-start | bytes 24580
  471.8 10.9 %copy-start.1 = (bf16[256,2304]{1,0:T(8,128)(2,1)S(1)}, bf16[256,2304]{1,0:T(8,128)(2,1)}, u32[]{:S(2)}) copy-start(bf16[256,2304]{1,0:T(8,128)(2,1)} %fusion.4) | copy-start | bytes 3538948
  482.7 85.6 %copy-start = (bf16[1,16,16,2048]{3,2,1,0:T(8,128)(2,1)S(1)}, bf16[1,16,16,2048]{3,2,1,0:T(8,128)(2,1)}, u32[]{:S(2)}) copy-start(bf16[1,16,16,2048]{3,2,1,0:T(8,128)(2,1)} %param.5) | copy-start | bytes 3145732
Sparse Core Ops, SparseCore 0:
  12.0 59.8 all-gather.2
  79.7 392.0 all-gather.4
  481.6 85.7 reduce-scatter.1
where the time goes:
time: 623 us
  waiting for transfers between devices  521 us (84%)
  blocking collectives  45.8 us (7%)
  other arithmetic  20.9 us (3%)
  matrix products  17.2 us (3%)
  between operations  16.5 us (3%)
    all_gather x1, waiting for transfers between devices, on_device(): lax.all_gather(learner_score_matrix, 'mp', axis=0, tiled=True)  382 us
    reduce_scatter x1, waiting for transfers between devices, on_device(): lax.psum_scatter(lax.dot_general(score_derivative, weights, (((1,), (1,))...  79.3 us
    all_gather x1, waiting for transfers between devices, on_device(): lax.all_gather(pooled, 'fsdp', axis=0, tiled=True)  60 us
    unnamed x1, blocking collectives  45.8 us
  transfers between devices with their start and end apart: 3, of which 3 were waited for; matrix products, arithmetic and copies ran while one was open for 2% of the time, Pallas kernels for 0%

commit v1 on v0

v1 whole, which is shorter than its diff:
```python
import functools
import math

import jax
import jax.numpy as jnp
from jax import lax
from jax.experimental import pallas as pl
from jax.experimental.pallas import tpu as pltpu
from jax.sharding import PartitionSpec as P

MESH = pl.DeviceIdType.MESH
EPS = 1e-05
LC = 768
ROWS = 16
ORDER = ((0, 0), (1, 0), (1, 1), (0, 1))
SKEW = dict(edge=2, cross=4, back=6, ew=8, m2=10)


def kernel(
    K, steps_per, partner, gain, hidden, codes, head,
    out_hidden, out_loss, out_gain,
    hv, ht, pb, lg, db, dl, dp, rss, rsr, xs, es, ns, inv, la, ls, lr, lrr,
    cb, cr, clb, clr, acc, accl, tg, gg, rank, sel, *rest,
):
    S = 4 * steps_per
    za, zc = rest[:S], rest[S : 2 * S]
    (hsem, ag_s, ag_r, y_s, y_r, z_s, z_r, b_s, b_r, l_s, l_r, r_s, r_r, q_s, q_r, c_s, c_r, g_s, g_r) = rest[2 * S :]
    mp, f = lax.axis_index("mp"), lax.axis_index("fsdp")
    y, z = mp // 4, lax.rem(mp, 4)
    h, x, core = f // 8, lax.rem(f, 8) // 2, lax.rem(f, 2)
    half = z // 2
    edge = lax.rem(z + 1, 4) < 2
    inner = jnp.logical_not(edge)
    zin, zout = 1 + half, 3 * half
    sends = []

    def start(src, dst, ssem, rsem, dev, when=None):
        def go():
            pltpu.make_async_remote_copy(src, dst, ssem, rsem, device_id=dev, device_id_type=MESH).start()

        def end():
            pltpu.make_async_remote_copy(src, dst, ssem, rsem, device_id=dev, device_id_type=MESH).wait_send()

        if when is None:
            go()
            sends.append(end)
        else:
            pl.when(when)(go)
            sends.append(lambda: pl.when(when)(end))

    def arrived(dst, rsem, when=None):
        def go():
            pltpu.make_async_remote_copy(dst, dst, rsem, rsem, device_id={"mp": mp, "fsdp": lax.rem(f + 1, 16)}, device_id_type=MESH).wait_recv()

        if when is None:
            go()
        else:
            pl.when(when)(go)

    def ydev(d):
        return lax.rem(y + d, 4)

    loads = []
    for lc in range(steps_per):
        c = pltpu.make_async_copy(head.at[0, :, pl.ds(lc * LC, LC)], hv.at[lc], hsem.at[lc])
        c.start()
        loads.append(c)

    bar = pltpu.get_barrier_semaphore()
    for i in range(1, 16):
        pl.semaphore_signal(bar, inc=1, device_id={"fsdp": lax.rem(f + i, 16)}, device_id_type=MESH)
    for d in (1, 2, 3):
        pl.semaphore_signal(bar, inc=1, device_id={"mp": ydev(d) * 4 + z}, device_id_type=MESH)

    @pl.when(edge)
    def _():
        pl.semaphore_signal(bar, inc=1, device_id={"mp": y * 4 + zin}, device_id_type=MESH)

    @pl.when(inner)
    def _():
        pl.semaphore_signal(bar, inc=1, device_id={"mp": y * 4 + zout}, device_id_type=MESH)
        pl.semaphore_signal(bar, inc=1, device_id={"mp": y * 4 + 3 - z}, device_id_type=MESH)

    def pool(n, _):
        states = hidden[0, n].astype(jnp.float32)
        r = lax.rsqrt(jnp.mean(states * states, axis=-1, keepdims=True) + EPS)
        inv[n] = jnp.broadcast_to(r, (16, 128))
        ns[pl.ds(n, 1), :] = jnp.sum(states * r, axis=0, keepdims=True)
        return 0

    lax.fori_loop(0, ROWS, pool, 0)
    pb[core, x] = (ns[...] * gain[...] * 0.25).astype(jnp.bfloat16)

    for hh in range(2):
        r = jnp.int32(0)
        for o in range(8):
            m = 4 * (o % 4) + (1 + hh if o < 4 else 3 * hh)
            rank[m] = r
            r = r + (((partner[m] & 3) >> 1) ^ hh)

    def place(p):
        pz, py = p & 3, p >> 2
        return jnp.where(pz == zin, py, jnp.where(pz == zout, 4 + py, 8 + rank[p]))

    for j in range(4):
        p = partner[4 * j + z]
        sel[j] = jnp.where(edge, jnp.where((p & 3) == z, p >> 2, 4 + j), place(p))
        p = partner[4 * j + zout]
        sel[4 + j] = jnp.where((p & 3) == zout, 0, place(p))
    picks = [jnp.int32(0)] * K
    for o in range(8):
        m = 4 * (o % 4) + (zin if o < 4 else zout)
        away = ((partner[m] & 3) >> 1) != half
        for j in range(K):
            picks[j] = jnp.where(jnp.logical_and(away, rank[m] == j), o, picks[j])
    for j in range(K):
        sel[8 + j] = picks[j]

    @pl.when(edge)
    def _():
        pl.semaphore_wait(bar, 19)

    @pl.when(inner)
    def _():
        pl.semaphore_wait(bar, 20)

    def mates(c, lo, when):
        i = lo
        for dx, dc in ((0, 1), (1, 0), (3, 0), (1, 1), (3, 1), (2, 0), (2, 1)):
            dev = {"fsdp": h * 8 + lax.rem(x + dx, 4) * 2 + lax.rem(core + dc, 2)}
            start(pb.at[c, x], pb.at[c, x], ag_s.at[i], ag_r.at[c, x], dev, when)
            i += 1

    other = {"fsdp": lax.rem(f + 8, 16)}
    start(pb.at[core, x], pb.at[2 + core, x], ag_s.at[0], ag_r.at[2 + core, x], other)
    mates(core, 1, core == 0)

    for lc in range(steps_per):
        loads[lc].wait()

        def turn(i, _):
            r = pl.multiple_of(i * 256, 256)
            ht[lc, :, pl.ds(r, 256)] = hv[lc, pl.ds(r, 256), :].T
            return 0

        lax.fori_loop(0, 8, turn, 0)

    def stage_m1(s):
        ci, lc = s // steps_per, s % steps_per
        rel, cc = ORDER[ci]
        c = rel * 2 + cc
        if lc == 0:
            for i in range(4):
                mine = jnp.logical_and(core == cc, x == i)
                arrived(pb.at[c, i], ag_r.at[c, i], jnp.logical_not(mine))
        v = jnp.dot(pb[c].reshape(64, pb.shape[3]), hv[lc], preferred_element_type=jnp.float32).astype(jnp.bfloat16)
        for i in range(4):
            lg[s, i] = v[i * 16 : (i + 1) * 16]
        za[s][y] = lg[s, y]
        for d in (1, 3, 2):
            start(lg.at[s, ydev(d)], za[s].at[y], y_s.at[s, d], y_r.at[s, y], {"mp": ydev(d) * 4 + z})

    def stage_edge(s):
        for d in (1, 3, 2):
            arrived(za[s].at[ydev(d)], y_r.at[s, ydev(d)])
        start(za[s].at[pl.ds(0, 4)], za[s].at[pl.ds(4, 4)], z_s.at[s, 0], z_r.at[s, 0], {"mp": y * 4 + zin}, edge)

    def fetch(s, i):
        a = za[s][jnp.minimum(i, 7)]
        b = zc[s][jnp.maximum(i - 8, 0)]
        return jnp.where(i < 8, a, b)

    def stage_cross(s):
        @pl.when(inner)
        def _():
            arrived(za[s].at[pl.ds(4, 4)], z_r.at[s, 0])
            for j in range(K):
                xs[s, j] = za[s][sel[8 + j]]

        start(xs.at[s], zc[s], z_s.at[s, 1], z_r.at[s, 1], {"mp": y * 4 + 3 - z}, inner)

    def stage_back(s):
        @pl.when(inner)
        def _():
            arrived(zc[s], z_r.at[s, 1])
            for j in range(4):
                es[s, j] = fetch(s, sel[4 + j])

        start(es.at[s], za[s].at[pl.ds(4, 4)], z_s.at[s, 0], z_r.at[s, 0], {"mp": y * 4 + zout}, inner)

    def stage_ew(s):
        ci, lc = s // steps_per, s % steps_per
        rel, cc = ORDER[ci]
        arrived(za[s].at[pl.ds(4, 4)], z_r.at[s, 0], edge)
        hc = h if rel == 0 else 1 - h
        row = pl.multiple_of((hc * 8 + y * 2 + cc) * 16, 16)
        ids = codes[pl.ds(row, 16), :] - (f * (LC * steps_per) + lc * LC)
        lanes = lax.broadcasted_iota(jnp.int32, (16, LC), 1)
        hit = ids[:, 0:1] == lanes
        for j in range(1, 16):
            hit = jnp.logical_or(hit, ids[:, j : j + 1] == lanes)
        tg[...] = jnp.where(hit, 1.0, 0.0)

        def model(j, _):
            i = sel[j]
            a = za[s][jnp.minimum(i, 7)]
            b = zc[s][jnp.maximum(i - 8, 0)]
            q = jnp.where(i < 8, a, b).astype(jnp.float32)
            v = za[s][j].astype(jnp.float32)
            target = tg[...]
            e = jnp.exp(jnp.abs(v) * -0.5)
            e2 = e * e
            a1, b1 = 1.0 + e, 1.0 + e2
            rr = 1.0 / (a1 * b1)
            pos = v >= 0.0
            s12 = (jnp.where(pos, 1.0, e2) * a1 + jnp.where(pos, 1.0, e) * b1) * rr
            t = 1.0 / (1.0 + jnp.exp(q * -0.5))
            db[s, j] = (s12 - target - t).astype(jnp.bfloat16)
            each = 2.0 * jnp.maximum(v, 0.0) + jnp.log(a1 * a1 * b1) - (t + target) * v
            part = each[:, 0:128]
            for k in range(128, LC, 128):
                part = part + each[:, k : k + 128]
            if lc == 0:
                la[ci, j] = part
            else:
                la[ci, j] += part
            return 0

        lax.fori_loop(0, 4, model, 0)
        dl[s, y] = db[s, y]
        for d in (1, 3, 2):
            start(db.at[s, ydev(d)], dl.at[s, y], b_s.at[s, d], b_r.at[s, y], {"mp": ydev(d) * 4 + z})
        if lc == steps_per - 1:
            diag = lax.broadcasted_iota(jnp.int32, (16, 128), 0) == lax.broadcasted_iota(jnp.int32, (16, 128), 1)
            for j in range(4):
                total = jnp.sum(la[ci, j], axis=1, keepdims=True)
                line = jnp.sum(jnp.where(diag, total, 0.0), axis=0, keepdims=True)
                ls[ci, j] = jnp.broadcast_to(line, (8, 128))
            lr[ci, y] = ls[ci, y]
            for d in (1, 3, 2):
                start(ls.at[ci, ydev(d)], lr.at[ci, y], l_s.at[ci, d], l_r.at[ci, y], {"mp": ydev(d) * 4 + z})

    def stage_m2(s):
        ci, lc = s // steps_per, s % steps_per
        rel, cc = ORDER[ci]
        c = rel * 2 + cc
        for d in (1, 3, 2):
            arrived(dl.at[s, ydev(d)], b_r.at[s, ydev(d)])
        left = dl[s].reshape(64, LC)
        for n in range(0, 2048, 1024):
            v = jnp.dot(left, ht[lc, :, n : n + 1024], preferred_element_type=jnp.float32)
            for i in range(4):
                w = v[i * 16 : (i + 1) * 16]
                if lc > 0:
                    w = w + dp[c, i, :, n : n + 1024]
                dp[c, i, :, n : n + 1024] = w
                if lc == steps_per - 1:
                    rss[ci, i, :, n : n + 1024] = w.astype(jnp.bfloat16)
        if lc == steps_per - 1:
            me = x * 2 + core
            for dx in (1, 3, 2, 0):
                xx = lax.rem(x + dx, 4)
                dev = {"fsdp": h * 8 + xx * 2 + cc}
                when = None if dx else core != cc
                start(rss.at[ci, xx], rsr.at[rel, me], r_s.at[ci, dx], r_r.at[rel, me], dev, when)
            for d in (1, 3, 2):
                arrived(lr.at[ci, ydev(d)], l_r.at[ci, ydev(d)])
            for dx in (1, 3, 2, 0):
                xx = lax.rem(x + dx, 4)
                dev = {"fsdp": h * 8 + xx * 2 + cc}
                when = None if dx else core != cc
                start(lr.at[ci, xx], lrr.at[rel, me], q_s.at[ci, dx], q_r.at[rel, me], dev, when)

    def gather_sum(rel):
        ci = jnp.where(core == 0, ORDER.index((rel, 0)), ORDER.index((rel, 1)))
        me = x * 2 + core
        acc[...] = dp[rel * 2 + core, x]
        accl[...] = lr[ci, x]
        for i in range(1, 8):
            src = lax.rem(me + i, 8)
            arrived(rsr.at[rel, src], r_r.at[rel, src])
            acc[...] += rsr[rel, src].astype(jnp.float32)
        for i in range(1, 8):
            src = lax.rem(me + i, 8)
            arrived(lrr.at[rel, src], q_r.at[rel, src])
            accl[...] += lrr[rel, src]

    for t in range(S + SKEW["m2"]):
        if t < S:
            stage_m1(t)
        if t == steps_per - 1:
            arrived(pb.at[2 + core, x], ag_r.at[2 + core, x])
            mates(2 + core, 8, None)
            mates(core, 1 + 14, core == 1)
        for name, fn in (("edge", stage_edge), ("cross", stage_cross), ("back", stage_back), ("ew", stage_ew), ("m2", stage_m2)):
            s = t - SKEW[name]
            if 0 <= s < S:
                fn(s)
                if name == "m2" and s == S - 2:
                    gather_sum(1)
                    cb[...] = acc[...].astype(jnp.bfloat16)
                    clb[...] = accl[...]
                    start(cb, cr, c_s.at[0], c_r.at[0], other)
                    start(clb, clr, c_s.at[1], c_r.at[1], other)

    gather_sum(0)
    arrived(cr, c_r.at[0])
    arrived(clr, c_r.at[1])
    acc[...] = (acc[...] + cr[...].astype(jnp.float32)) * 0.25
    out_loss[...] = (accl[...] + clr[...]) * (1.0 / (LC * steps_per * 16))
    gg[f] = jnp.sum(acc[...] * ns[...], axis=0, keepdims=True)
    for i in range(1, 16):
        start(gg.at[f], gg.at[f], g_s.at[i], g_r.at[f], {"fsdp": lax.rem(f + i, 16)})

    def final(n, _):
        dn = acc[pl.ds(n, 1), :] * gain[...]
        r = inv[n][:, 0:1]
        nm = hidden[0, n].astype(jnp.float32) * r
        mean = jnp.mean(dn * nm, axis=-1, keepdims=True)
        out_hidden[0, n] = (r * (dn - nm * mean)).astype(jnp.bfloat16)
        return 0

    lax.fori_loop(0, ROWS, final, 0)
    for i in range(1, 16):
        src = lax.rem(f + i, 16)
        arrived(gg.at[src], g_r.at[src])
    total = gg[0]
    for i in range(1, 16):
        total = total + gg[i]
    out_gain[...] = total
    for end in sends:
        end()


def call(K, cid, hidden, gain, head, partner, codes):
    D = hidden.shape[3]
    steps_per = head.shape[2] // LC
    S = 4 * steps_per
    bf, f32 = jnp.bfloat16, jnp.float32
    V, dma = pltpu.VMEM, pltpu.SemaphoreType.DMA
    vmem = pl.BlockSpec(memory_space=pltpu.VMEM)
    scratch = [
        V((steps_per, D, LC), bf), V((steps_per, LC, D), bf), V((4, 4, 16, D), bf),
        V((S, 4, 16, LC), bf), V((S, 4, 16, LC), bf), V((S, 4, 16, LC), bf),
        V((4, 4, 16, D), f32), V((4, 4, 16, D), bf), V((2, 8, 16, D), bf),
        V((S, K, 16, LC), bf), V((S, 4, 16, LC), bf),
        V((16, D), f32), V((16, 16, 128), f32), V((4, 4, 16, 128), f32),
        V((4, 4, 8, 128), f32), V((4, 4, 8, 128), f32), V((2, 8, 8, 128), f32),
        V((16, D), bf), V((16, D), bf), V((8, 128), f32), V((8, 128), f32),
        V((16, D), f32), V((8, 128), f32), V((16, LC), f32), V((16, 1, D), f32),
        pltpu.SMEM((16,), jnp.int32), pltpu.SMEM((8 + K,), jnp.int32),
    ]
    scratch += [V((8, 16, LC), bf) for _ in range(S)]
    scratch += [V((K, 16, LC), bf) for _ in range(S)]
    scratch += [
        dma((steps_per,)), dma((22,)), dma((4, 4)), dma((S, 4)), dma((S, 4)), dma((S, 2)), dma((S, 2)),
        dma((S, 4)), dma((S, 4)), dma((4, 4)), dma((4, 4)), dma((4, 4)), dma((2, 8)), dma((4, 4)), dma((2, 8)),
        dma((2,)), dma((2,)), dma((16,)), dma((16,)),
    ]
    return pl.pallas_call(
        functools.partial(kernel, K, steps_per),
        name="distill%d" % K,
        out_shape=(
            jax.ShapeDtypeStruct(hidden.shape, bf),
            jax.ShapeDtypeStruct((8, 128), f32),
            jax.ShapeDtypeStruct((1, D), f32),
        ),
        in_specs=[pl.BlockSpec(memory_space=pltpu.SMEM), vmem, vmem, vmem, pl.BlockSpec(memory_space=pl.ANY)],
        out_specs=(vmem, vmem, vmem),
        scratch_shapes=scratch,
        compiler_params=pltpu.CompilerParams(
            collective_id=cid, has_side_effects=True, vmem_limit_bytes=60 * 2**20
        ),
    )(partner, gain, hidden, codes, head)


def on_device(hidden, gain, head, partner, codes):
    grad_hidden, loss, grad_gain = call(8, 1, hidden, gain, head, partner, codes)
    return grad_hidden, loss[0:1, 0:16], grad_gain


def solution(mesh):
    return jax.shard_map(
        on_device,
        mesh=mesh,
        in_specs=(P("mp", "fsdp", None, None), P("mp", None), P("mp", None, "fsdp"), P(), P()),
        out_specs=(P("mp", "fsdp", None, None), P("mp", "fsdp"), P("mp", None)),
        check_vma=False,
    )
```

time: 623 us -> 113 us (0.18)
  waiting for transfers between devices: 521 us -> 0 us
  Pallas kernels: 0 us -> 106 us
  blocking collectives: 45.8 us -> 0 us
  other arithmetic: 20.9 us -> 0 us
  matrix products: 17.2 us -> 0 us
  between operations: 16.5 us -> 0.64 us
    all_gather x2 -> x0, waiting for transfers between devices: 442 us -> none  [the longest x1 382 us: on_device(): lax.all_gather(learner_score_matrix, 'mp', axis=0, tiled=True)]
    pallas_call x0 -> x1, Pallas kernels: none -> 106 us  [call(): pl.pallas_call(functools.partial(kernel, K, steps_per), name='distill%d'...]
    reduce_scatter x1 -> x0, waiting for transfers between devices: 79.3 us -> none  [on_device(): lax.psum_scatter(lax.dot_general(score_derivative, weights, (((1,), (1,))...]
    unnamed x1 -> x0, blocking collectives: 45.8 us -> none
    dot_general x2 -> x0, matrix products: 17.2 us -> none  [the longest x1 9.62 us: on_device(): lax.dot_general(score_derivative, weights, (((1,), (1,)), ((), ())), pref...]
    reduce_sum x5 -> x0, other arithmetic: 9.96 us -> none  [the longest x1 5.33 us: on_device(): jnp.sum(combined_cost_sum, axis=1)]
    reduce_or x1 -> x0, other arithmetic: 7.57 us -> none  [on_device(): jnp.any(codes[:, :, None] == label_ids[None, None, :], axis=1)]
  transfers between devices with their start and end apart: 3 -> 0, of which waited for: 3 -> 0; matrix products, arithmetic and copies ran while one was open for 2% -> 0% of each run, Pallas kernels for 0% -> 0%
where the time goes in v1:
time: 113 us
  Pallas kernels  106 us (94%)
  local copies, waits for them, and re-layouts  6.25 us (6%)
    pallas_call x1, Pallas kernels, call(): pl.pallas_call(functools.partial(kernel, K, steps_per), name='distill%d'...  106 us
    unnamed x3, local copies, waits for them, and re-layouts  5.07 us

profile of v1, /device:TPU:1, one launch (start us, length us, event | category | flops | bytes accessed | tf_op | source)
XLA Modules:
  0.0 112.5 jit_solution(3394549365567823355)
XLA Ops:
  0.6 1.5 %copy.8.codes = s32[256,16]{1,0:T(8,128)} copy(s32[256,16]{0,1:T(8,128)} %param.9) | data formatting | bytes 32768 | tf_op args[4]
  2.1 105.6 %distill8.1 = (bf16[1,16,16,2048]{3,2,1,0:T(8,128)(2,1)}, f32[8,128]{1,0:T(8,128)}, f32[1,2048]{1,0:T(1,128)}) custom-call(s32[16]{0:T(128)} %partner.1, f32[1,2048]{1,0:T(1,128)} %gain.1, bf16[1,16,16,2048]{3,2,1,0:T(8,128)(2,1)} %hidden.1, s32[256,16]{1,0:T(8,128)} %copy.8.codes, bf16[1,2048,2304]{2,1,0:T(8,128)(2,1)} %head.1), custom_call_target="tpu_custom_call" | custom-call | tf_op jit(solution)/shard_map/distill8/pallas_call | solution.py:360
  107.7 1.2 %slice.3 = f32[1,16]{1,0:T(1,128)} slice(f32[8,128]{1,0:T(8,128)} %get-tuple-element.7), slice={[0:1], [0:16]} | slice | bytes 128 | tf_op jit(solution)/shard_map/slice | solution.py:379
  108.9 2.3 %copy.11 = bf16[1,16,16,2048]{3,2,1,0:T(8,128)(2,1)} copy(bf16[1,16,16,2048]{3,2,1,0:T(8,128)(2,1)} %get-tuple-element.12) | data formatting | bytes 2097152
  111.2 1.3 %copy.12 = f32[1,2048]{1,0:T(1,128)} copy(f32[1,2048]{1,0:T(1,128)} %get-tuple-element.14) | data formatting | bytes 16384

commit v2 on v0

v2 whole, which is shorter than its diff:
```python
import functools
import math

import jax
import jax.numpy as jnp
from jax import lax
from jax.experimental import pallas as pl
from jax.experimental.pallas import tpu as pltpu
from jax.sharding import PartitionSpec as P

MESH = pl.DeviceIdType.MESH
EPS = 1e-05
LC = 768
ROWS = 16
SIZES = (4, 8)
EDGE, CROSS, BACK, EW, M2 = 2, 4, 6, 8, 10


def kernel(
    K, per, partner, gain, codes, hidden, head,
    out_acc, out_loss, out_gain, inv,
    hs, ct, hv, ht, pb, lg, db, dl, dp, rss, rsr, xs, es, ns, la, ls, lr, lrr,
    cb, cr, clb, clr, accl, tg, gg, za, zc, rank, sel,
    isem, hsem, ag_s, ag_r, y_s, y_r, z_s, z_r, b_s, b_r, l_s, l_r, r_s, r_r, q_s, q_r, c_s, c_r, g_s, g_r,
):
    S = 4 * per
    mp, f = lax.axis_index("mp"), lax.axis_index("fsdp")
    y, z = mp // 4, lax.rem(mp, 4)
    h, x, core = f // 8, lax.rem(f, 8) // 2, lax.rem(f, 2)
    half = z // 2
    edge = lax.rem(z + 1, 4) < 2
    inner = jnp.logical_not(edge)
    zin, zout = 1 + half, 3 * half
    me = x * 2 + core
    other = {"fsdp": lax.rem(f + 8, 16)}
    sibling = {"fsdp": f + 1 - 2 * core}

    def remote(src, dst, ssem, rsem, dev):
        return pltpu.make_async_remote_copy(src, dst, ssem, rsem, device_id=dev, device_id_type=MESH)

    def start(*copy):
        remote(*copy).start()

    def arrived(dst, rsem):
        remote(dst, dst, rsem, rsem, other).wait_recv()

    def sent(src, ssem):
        remote(src, src, ssem, ssem, other).wait_send()

    def loop(n, body):
        def step(i, _):
            body(i)
            return 0

        lax.fori_loop(0, n, step, 0)

    def chunk(ci):
        return lax.rem((ci + 1) // 2, 2), ci // 2

    def ydev(d):
        return lax.rem(y + d, 4)

    def mate(d):
        return {"mp": ydev(d) * 4 + z}

    whole_hidden = pltpu.make_async_copy(hidden.at[0], hs, isem)
    whole_hidden.start()

    def head_part(lc):
        return pltpu.make_async_copy(head.at[0, :, pl.ds(pl.multiple_of(lc * LC, 128), LC)], hv.at[lc], hsem.at[lc])

    loop(per, lambda lc: head_part(lc).start())

    bar = pltpu.get_barrier_semaphore()

    def greet(dev):
        pl.semaphore_signal(bar, inc=1, device_id=dev, device_id_type=MESH)

    loop(15, lambda i: greet({"fsdp": lax.rem(f + i + 1, 16)}))
    loop(3, lambda i: greet(mate(i + 1)))

    @pl.when(edge)
    def _():
        greet({"mp": y * 4 + zin})

    @pl.when(inner)
    def _():
        greet({"mp": y * 4 + zout})
        greet({"mp": y * 4 + 3 - z})

    for hh in range(2):
        r = jnp.int32(0)
        for o in range(8):
            m = 4 * (o % 4) + (1 + hh if o < 4 else 3 * hh)
            rank[m] = r
            r = r + (((partner[m] & 3) >> 1) ^ hh)

    def place(p):
        pz, py = p & 3, p >> 2
        return jnp.where(pz == zin, py, jnp.where(pz == zout, 4 + py, 8 + rank[p]))

    def find(j):
        p = partner[4 * j + z]
        sel[j] = jnp.where(edge, jnp.where((p & 3) == z, p >> 2, 4 + j), place(p))
        p = partner[4 * j + zout]
        sel[4 + j] = jnp.where((p & 3) == zout, 0, place(p))

    loop(4, find)

    def pick(j):
        got = jnp.int32(0)
        for o in range(8):
            m = 4 * (o % 4) + (zin if o < 4 else zout)
            away = ((partner[m] & 3) >> 1) != half
            got = jnp.where(jnp.logical_and(away, rank[m] == j), o, got)
        sel[8 + j] = got

    loop(K, pick)

    whole_hidden.wait()

    def pool(n, _):
        states = hs[n].astype(jnp.float32)
        r = lax.rsqrt(jnp.mean(states * states, axis=-1, keepdims=True) + EPS)
        inv[n] = jnp.broadcast_to(r, (16, 128))
        ns[pl.ds(n, 1), :] = jnp.sum(states * r, axis=0, keepdims=True)
        return 0

    lax.fori_loop(0, ROWS, pool, 0, unroll=4)
    pb[core, x] = (ns[...] * gain[...] * 0.25).astype(jnp.bfloat16)

    @pl.when(edge)
    def _():
        pl.semaphore_wait(bar, 19)

    @pl.when(inner)
    def _():
        pl.semaphore_wait(bar, 20)

    def spread(c, i):
        for k, dx in enumerate((1, 3, 2)):
            start(pb.at[c, x], pb.at[c, x], ag_s.at[i + k], ag_r.at[c, x], {"fsdp": h * 8 + lax.rem(x + dx, 4) * 2 + core})
        start(pb.at[c, x], pb.at[c, x], ag_s.at[i + 3], ag_r.at[c, x], sibling)

    def hand_on(c, i):
        for k, dx in enumerate((1, 3, 2)):
            xx = lax.rem(x + dx, 4)
            arrived(pb.at[c, xx], ag_r.at[c, xx])
            start(pb.at[c, xx], pb.at[c, xx], ag_s.at[i + k], ag_r.at[c, xx], sibling)

    start(pb.at[core, x], pb.at[2 + core, x], ag_s.at[0], ag_r.at[2 + core, x], other)
    spread(core, 1)

    ct[...] = codes[...].T
    la[...] = jnp.zeros_like(la)
    gg[f] = jnp.zeros_like(gg[f])

    def clear(i):
        dp[i // 4, lax.rem(i, 4)] = jnp.zeros(dp.shape[2:], jnp.float32)

    loop(16, clear)

    def turn(lc):
        head_part(lc).wait()

        def part(i):
            r = pl.multiple_of(i * 256, 256)
            ht[lc, :, pl.ds(r, 256)] = hv[lc, pl.ds(r, 256), :].T

        loop(8, part)

        @pl.when(lc == 0)
        def _():
            hand_on(core, 5)

    loop(per, turn)

    def stage_m1(s):
        ci = s // per
        lc = s - ci * per
        rel, cc = chunk(ci)
        c = rel * 2 + cc

        @pl.when(jnp.logical_and(lc == 0, core != cc))
        def _():
            loop(4, lambda i: arrived(pb.at[c, i], ag_r.at[c, i]))

        v = jnp.dot(pb[c].reshape(64, pb.shape[3]), hv[lc], preferred_element_type=jnp.float32).astype(jnp.bfloat16)
        for i in range(4):
            lg[s, i] = v[i * 16 : (i + 1) * 16]
        za[s, y] = lg[s, y]
        for d in (1, 3, 2):
            start(lg.at[s, ydev(d)], za.at[s, y], y_s.at[s, d], y_r.at[s, y], mate(d))

    def outer(s):
        return za.at[s, pl.ds(4, 4)]

    def stage_edge(s):
        loop(3, lambda i: arrived(za.at[s, ydev(i + 1)], y_r.at[s, ydev(i + 1)]))

        @pl.when(edge)
        def _():
            start(za.at[s, pl.ds(0, 4)], outer(s), z_s.at[s, 0], z_r.at[s, 0], {"mp": y * 4 + zin})

    def fetch(s, i, n):
        got = za[s, 0]
        for k in range(1, n):
            got = jnp.where(i == k, za[s, k] if k < 8 else zc[s, k - 8], got)
        return got

    def stage_cross(s):
        @pl.when(inner)
        def _():
            arrived(outer(s), z_r.at[s, 0])

            def put(j):
                xs[s, j] = fetch(s, sel[8 + j], 8)

            loop(K, put)
            start(xs.at[s], zc.at[s], z_s.at[s, 1], z_r.at[s, 1], {"mp": y * 4 + 3 - z})

    def stage_back(s):
        @pl.when(inner)
        def _():
            arrived(zc.at[s], z_r.at[s, 1])

            def put(j):
                es[s, j] = fetch(s, sel[4 + j], 8 + K)

            loop(4, put)
            start(es.at[s], outer(s), z_s.at[s, 0], z_r.at[s, 0], {"mp": y * 4 + zout})

    def stage_ew(s):
        ci = s // per
        lc = s - ci * per
        rel, cc = chunk(ci)

        @pl.when(edge)
        def _():
            arrived(outer(s), z_r.at[s, 0])

        hc = jnp.where(rel == 0, h, 1 - h)
        row = pl.multiple_of((hc * 8 + y * 2 + cc) * 16, 16)
        ids = ct[pl.ds(row, 16), :] - (f * (LC * per) + lc * LC)
        lanes = lax.broadcasted_iota(jnp.int32, (16, LC), 1)
        hit = ids[:, 0:1] == lanes
        for j in range(1, 16):
            hit = jnp.logical_or(hit, ids[:, j : j + 1] == lanes)
        tg[...] = jnp.where(hit, 1.0, 0.0)

        def model(j):
            q = fetch(s, sel[j], 8 + K).astype(jnp.float32)
            v = za[s, j].astype(jnp.float32)
            target = tg[...]
            e = jnp.exp(jnp.abs(v) * -0.5)
            e2 = e * e
            a1, b1 = 1.0 + e, 1.0 + e2
            rr = 1.0 / (a1 * b1)
            pos = v >= 0.0
            s12 = (jnp.where(pos, 1.0, e2) * a1 + jnp.where(pos, 1.0, e) * b1) * rr
            t = 1.0 / (1.0 + jnp.exp(q * -0.5))
            db[s, j] = (s12 - target - t).astype(jnp.bfloat16)
            each = 2.0 * jnp.maximum(v, 0.0) + jnp.log(a1 * a1 * b1) - (t + target) * v
            part = each[:, 0:128]
            for k in range(128, LC, 128):
                part = part + each[:, k : k + 128]
            la[ci, j] += part

        loop(4, model)
        dl[s, y] = db[s, y]
        for d in (1, 3, 2):
            start(db.at[s, ydev(d)], dl.at[s, y], b_s.at[s, d], b_r.at[s, y], mate(d))

        @pl.when(lc == per - 1)
        def _():
            diag = lax.broadcasted_iota(jnp.int32, (16, 128), 0) == lax.broadcasted_iota(jnp.int32, (16, 128), 1)

            def line(j):
                total = jnp.sum(la[ci, j], axis=1, keepdims=True)
                row = jnp.sum(jnp.where(diag, total, 0.0), axis=0, keepdims=True)
                ls[ci, j] = jnp.broadcast_to(row, (8, 128))

            loop(4, line)
            lr[ci, y] = ls[ci, y]
            for d in (1, 3, 2):
                start(ls.at[ci, ydev(d)], lr.at[ci, y], l_s.at[ci, d], l_r.at[ci, y], mate(d))

    def owner(dx, cc):
        xx = lax.rem(x + dx, 4)
        return xx, {"fsdp": h * 8 + xx * 2 + cc}

    def stage_m2(s):
        ci = s // per
        lc = s - ci * per
        rel, cc = chunk(ci)
        c = rel * 2 + cc
        loop(3, lambda i: arrived(dl.at[s, ydev(i + 1)], b_r.at[s, ydev(i + 1)]))
        left = dl[s].reshape(64, LC)
        for n in range(0, 2048, 1024):
            v = jnp.dot(left, ht[lc, :, n : n + 1024], preferred_element_type=jnp.float32)
            for i in range(4):
                dp[c, i, :, n : n + 1024] += v[i * 16 : (i + 1) * 16]

        @pl.when(lc == per - 1)
        def _():
            def turn_in(i):
                w = dp[c, i]
                rss[ci, i] = w.astype(jnp.bfloat16)
                gg[f] += jnp.sum(w * pb[c, i].astype(jnp.float32), axis=0, keepdims=True)

            loop(4, turn_in)

            def give(dx):
                xx, dev = owner(dx, cc)
                start(rss.at[ci, xx], rsr.at[rel, me], r_s.at[ci, dx], r_r.at[rel, me], dev)

            def give_loss(dx):
                xx, dev = owner(dx, cc)
                start(lr.at[ci, xx], lrr.at[rel, me], q_s.at[ci, dx], q_r.at[rel, me], dev)

            loop(3, lambda i: give(i + 1))
            pl.when(core != cc)(lambda: give(0))
            loop(3, lambda i: arrived(lr.at[ci, ydev(i + 1)], l_r.at[ci, ydev(i + 1)]))
            loop(3, lambda i: give_loss(i + 1))
            pl.when(core != cc)(lambda: give_loss(0))

    def gather_sum(rel):
        ci = jnp.where(core == 0, rel, 3 - rel)
        out_acc[...] = dp[rel * 2 + core, x]
        accl[...] = lr[ci, x]

        def add(i):
            src = lax.rem(me + 1 + i, 8)
            arrived(rsr.at[rel, src], r_r.at[rel, src])
            out_acc[...] += rsr[rel, src].astype(jnp.float32)
            arrived(lrr.at[rel, src], q_r.at[rel, src])
            accl[...] += lrr[rel, src]

        loop(7, add)

    def stage(t, lag, fn):
        pl.when(jnp.logical_and(t >= lag, t < S + lag))(lambda: fn(t - lag))

    def tick(t):
        pl.when(t < S)(lambda: stage_m1(t))

        @pl.when(t == 0)
        def _():
            arrived(pb.at[2 + core, x], ag_r.at[2 + core, x])
            spread(2 + core, 8)

        @pl.when(t == per - 1)
        def _():
            hand_on(2 + core, 12)

        stage(t, EDGE, stage_edge)
        stage(t, CROSS, stage_cross)
        stage(t, BACK, stage_back)
        stage(t, EW, stage_ew)
        stage(t, M2, stage_m2)

        @pl.when(t == S - 2 + M2)
        def _():
            gather_sum(1)
            cb[...] = out_acc[...].astype(jnp.bfloat16)
            clb[...] = accl[...]
            start(cb, cr, c_s.at[0], c_r.at[0], other)
            start(clb, clr, c_s.at[1], c_r.at[1], other)

    loop(S + M2, tick)

    loop(15, lambda i: start(gg.at[f], gg.at[f], g_s.at[i + 1], g_r.at[f], {"fsdp": lax.rem(f + 1 + i, 16)}))
    gather_sum(0)
    arrived(cr, c_r.at[0])
    arrived(clr, c_r.at[1])
    out_acc[...] = (out_acc[...] + cr[...].astype(jnp.float32)) * 0.25
    out_loss[...] = (accl[...] + clr[...]) * (1.0 / (LC * per * 16))
    out_gain[...] = gg[f]

    def add_gain(i):
        src = lax.rem(f + 1 + i, 16)
        arrived(gg.at[src], g_r.at[src])
        out_gain[...] += gg[src]

    loop(15, add_gain)
    out_gain[...] = out_gain[...] / gain[...]

    loop(15, lambda i: sent(pb.at[0, 0], ag_s.at[i]))
    loop(15, lambda i: sent(gg.at[f], g_s.at[i + 1]))
    sent(cb, c_s.at[0])
    sent(clb, c_s.at[1])

    def step_left(s):
        for d in (1, 2, 3):
            sent(lg.at[s, 0], y_s.at[s, d])
            sent(db.at[s, 0], b_s.at[s, d])
        sent(es.at[s], z_s.at[s, 0])
        pl.when(inner)(lambda: sent(xs.at[s], z_s.at[s, 1]))

    loop(S, step_left)

    def chunk_left(ci):
        def both(dx):
            sent(rss.at[ci, 0], r_s.at[ci, dx])
            sent(lr.at[ci, 0], q_s.at[ci, dx])

        for d in (1, 2, 3):
            sent(ls.at[ci, 0], l_s.at[ci, d])
            both(d)
        pl.when(core != ci // 2)(lambda: both(0))

    loop(4, chunk_left)


def call(K, cid, hidden, gain, head, partner, codes):
    D = hidden.shape[3]
    per = head.shape[2] // LC
    S = 4 * per
    bf, f32 = jnp.bfloat16, jnp.float32
    V, dma = pltpu.VMEM, pltpu.SemaphoreType.DMA
    vmem = pl.BlockSpec(memory_space=pltpu.VMEM)
    scratch = [
        V((16, 16, D), bf), V((256, 16), jnp.int32),
        V((per, D, LC), bf), V((per, LC, D), bf), V((4, 4, 16, D), bf),
        V((S, 4, 16, LC), bf), V((S, 4, 16, LC), bf), V((S, 4, 16, LC), bf),
        V((4, 4, 16, D), f32), V((4, 4, 16, D), bf), V((2, 8, 16, D), bf),
        V((S, K, 16, LC), bf), V((S, 4, 16, LC), bf),
        V((16, D), f32), V((4, 4, 16, 128), f32),
        V((4, 4, 8, 128), f32), V((4, 4, 8, 128), f32), V((2, 8, 8, 128), f32),
        V((16, D), bf), V((16, D), bf), V((8, 128), f32), V((8, 128), f32),
        V((8, 128), f32), V((16, LC), f32), V((16, 1, D), f32),
        V((S, 8, 16, LC), bf), V((S, K, 16, LC), bf),
        pltpu.SMEM((16,), jnp.int32), pltpu.SMEM((8 + K,), jnp.int32),
    ]
    scratch += [
        dma, dma((per,)), dma((15,)), dma((4, 4)), dma((S, 4)), dma((S, 4)), dma((S, 2)), dma((S, 2)),
        dma((S, 4)), dma((S, 4)), dma((4, 4)), dma((4, 4)), dma((4, 4)), dma((2, 8)), dma((4, 4)), dma((2, 8)),
        dma((2,)), dma((2,)), dma((16,)), dma((16,)),
    ]
    hbm = pl.BlockSpec(memory_space=pl.ANY)
    return pl.pallas_call(
        functools.partial(kernel, K, per),
        name="distill%d" % K,
        out_shape=(
            jax.ShapeDtypeStruct((16, D), f32),
            jax.ShapeDtypeStruct((8, 128), f32),
            jax.ShapeDtypeStruct((1, D), f32),
            jax.ShapeDtypeStruct((16, 16, 128), f32),
        ),
        in_specs=[pl.BlockSpec(memory_space=pltpu.SMEM), vmem, vmem, hbm, hbm],
        out_specs=(vmem, vmem, vmem, vmem),
        scratch_shapes=scratch,
        compiler_params=pltpu.CompilerParams(
            collective_id=cid, has_side_effects=True, vmem_limit_bytes=60 * 2**20
        ),
    )(partner, gain, codes, hidden, head)


def finish(acc, gain, inv, loss, total, hidden, out_hidden, out_loss, out_gain):
    g = gain[...]

    def note(n):
        dn = acc[n : n + 1, :] * g
        r = inv[n][:, 0:1]
        nm = hidden[0, n].astype(jnp.float32) * r
        mean = jnp.mean(dn * nm, axis=-1, keepdims=True)
        out_hidden[0, n] = (r * (dn - nm * mean)).astype(jnp.bfloat16)

    for n in range(8):
        note(n)

    @pl.when(pl.program_id(0) == 0)
    def _():
        out_loss[...] = loss[0:1, 0:16]
        out_gain[...] = total[...]


def last(acc, gain, inv, loss, total, hidden):
    D = hidden.shape[3]

    def whole(*shape):
        return pl.BlockSpec(shape, lambda i: (0,) * len(shape))

    block = pl.BlockSpec((1, 8, 16, D), lambda i: (0, i, 0, 0))
    return pl.pallas_call(
        finish,
        name="finish",
        grid=(2,),
        out_shape=(
            jax.ShapeDtypeStruct(hidden.shape, jnp.bfloat16),
            jax.ShapeDtypeStruct((1, 16), jnp.float32),
            jax.ShapeDtypeStruct((1, D), jnp.float32),
        ),
        in_specs=[
            pl.BlockSpec((8, D), lambda i: (i, 0)), whole(1, D), pl.BlockSpec((8, 16, 128), lambda i: (i, 0, 0)),
            whole(8, 128), whole(1, D), block,
        ],
        out_specs=(block, whole(1, 16), whole(1, D)),
    )(acc, gain, inv, loss, total, hidden)


def on_device(hidden, gain, head, partner, codes):
    ids = jnp.arange(16, dtype=jnp.int32)
    away = ((ids & 3) < 2) & ((partner & 3) >= 2)
    crossing = jnp.sum(away.astype(jnp.int32))
    args = (hidden, gain, head, partner, codes.T)
    calls = [functools.partial(call, K, i + 1) for i, K in enumerate(SIZES)]
    which = sum((crossing > K).astype(jnp.int32) for K in SIZES[:-1])
    acc, loss, total, inv = lax.switch(which, calls, *args) if len(SIZES) > 1 else calls[0](*args)
    return last(acc, gain, inv, loss, total, hidden)


def solution(mesh):
    return jax.shard_map(
        on_device,
        mesh=mesh,
        in_specs=(P("mp", "fsdp", None, None), P("mp", None), P("mp", None, "fsdp"), P(), P()),
        out_specs=(P("mp", "fsdp", None, None), P("mp", "fsdp"), P("mp", None)),
        check_vma=False,
    )
```

time: 623 us -> 85.4 us (0.14)
  waiting for transfers between devices: 521 us -> 0 us
  Pallas kernels: 0 us -> 82.6 us
  blocking collectives: 45.8 us -> 0 us
  other arithmetic: 20.9 us -> 1.3 us
  matrix products: 17.2 us -> 0 us
  between operations: 16.5 us -> 1.29 us
    all_gather x2 -> x0, waiting for transfers between devices: 442 us -> none  [the longest x1 382 us: on_device(): lax.all_gather(learner_score_matrix, 'mp', axis=0, tiled=True)]
    pallas_call x0 -> x2, Pallas kernels: none -> 82.6 us  [the longest x1 80 us: call(): pl.pallas_call(functools.partial(kernel, K, per), name='distill%d' % K, o...]
    reduce_scatter x1 -> x0, waiting for transfers between devices: 79.3 us -> none  [on_device(): lax.psum_scatter(lax.dot_general(score_derivative, weights, (((1,), (1,))...]
    unnamed x1 -> x0, blocking collectives: 45.8 us -> none
    dot_general x2 -> x0, matrix products: 17.2 us -> none  [the longest x1 9.62 us: on_device(): lax.dot_general(score_derivative, weights, (((1,), (1,)), ((), ())), pref...]
    reduce_sum x5 -> x1, other arithmetic: 9.96 us -> 1.3 us  [on_device(): crossing = jnp.sum(away.astype(jnp.int32))]
    reduce_or x1 -> x0, other arithmetic: 7.57 us -> none  [on_device(): jnp.any(codes[:, :, None] == label_ids[None, None, :], axis=1)]
  transfers between devices with their start and end apart: 3 -> 0, of which waited for: 3 -> 0; matrix products, arithmetic and copies ran while one was open for 2% -> 0% of each run, Pallas kernels for 0% -> 0%
where the time goes in v2:
time: 85.4 us; the launch traced here: 85.2 us
  Pallas kernels  82.6 us (97%)
  other arithmetic  1.3 us (2%)
  between operations  1.29 us (2%)
    pallas_call x1, Pallas kernels, call(): pl.pallas_call(functools.partial(kernel, K, per), name='distill%d' % K, o...  80 us
    pallas_call x1, Pallas kernels, last(): pl.pallas_call(finish, name='finish', grid=(2,), out_shape=(jax.ShapeDtyp...  2.59 us

profile of v2, /device:TPU:1, one launch (start us, length us, event | category | flops | bytes accessed | tf_op | source)
XLA Modules:
  0.0 85.2 jit_solution(13669292081664823022)
XLA Ops:
  0.6 1.3 %fusion = s32[]{:T(128)} fusion(s32[16]{0:T(128)} %param.10), kind=kLoop, calls=%fused_computation.1 | loop fusion | flops 111 | bytes 68 | tf_op jit(solution)/shard_map/reduce_sum | solution.py:505
  2.6 80.0 %conditional.1 = ((f32[16,2048]{1,0:T(8,128)S(1)}, f32[8,128]{1,0:T(8,128)S(1)}, f32[1,2048]{1,0:T(1,128)S(1)}, f32[16,16,128]{2,1,0:T(8,128)S(1)})) conditional(s32[]{:T(128)} %clamp.3, (s32[16]{0:T(128)}, f32[1,2048]{1,0:T(1,128)}, s32[16,256]{1,0:T(8,128)}, bf16[1,16,16,2048]{3,2,1,0:T(8,128)(2,1)}, bf16[1,2048,2304]{2,1,0:T(8,128)(2,1)}) %tuple.18, ...), branch_computations={%region_1.0_spmd, %region_2.0_spmd} | conditional | bytes 8 | solution.py:509
  2.6 80.0 %distill4.1 = (f32[16,2048]{1,0:T(8,128)S(1)}, f32[8,128]{1,0:T(8,128)S(1)}, f32[1,2048]{1,0:T(1,128)S(1)}, f32[16,16,128]{2,1,0:T(8,128)S(1)}) custom-call(s32[16]{0:T(128)} %get-tuple-element.20.partner, f32[1,2048]{1,0:T(1,128)} %get-tuple-element.21.gain, s32[16,256]{1,0:T(8,128)} %get-tuple-element.22.codes, ...), custom_call_target="tpu_custom_call" | custom-call | tf_op jit(solution)/shard_map/cond/branch_0_fun/distill4/pallas_call | solution.py:441
  82.6 2.6 %finish.1 = (bf16[1,16,16,2048]{3,2,1,0:T(8,128)(2,1)}, f32[1,16]{1,0:T(1,128)}, f32[1,2048]{1,0:T(1,128)}) custom-call(f32[16,2048]{1,0:T(8,128)S(1)} %get-tuple-element.37.acc, f32[1,2048]{1,0:T(1,128)} %gain.1, f32[16,16,128]{2,1,0:T(8,128)S(1)} %get-tuple-element.38.inv, f32[8,128]{1,0:T(8,128)S(1)} %get-tuple-element.39.loss, ...), custom_call_target="tpu_custom_call" | custom-call | tf_op jit(solution)/shard_map/finish/pallas_call | solution.py:485

commit v3 on v2

--- a/solution.py
+++ b/solution.py
@@ -12,8 +12,8 @@
 EPS = 1e-05
 LC = 768
 ROWS = 16
-SIZES = (4, 8)
-EDGE, CROSS, BACK, EW, M2 = 2, 4, 6, 8, 10
+SIZES = (4, 6, 8)
+EDGE, CROSS, BACK, EW, M2 = 2, 4, 6, 9, 11
 
 
 def kernel(
@@ -21,7 +21,7 @@
     out_acc, out_loss, out_gain, inv,
     hs, ct, hv, ht, pb, lg, db, dl, dp, rss, rsr, xs, es, ns, la, ls, lr, lrr,
     cb, cr, clb, clr, accl, tg, gg, za, zc, rank, sel,
-    isem, hsem, ag_s, ag_r, y_s, y_r, z_s, z_r, b_s, b_r, l_s, l_r, r_s, r_r, q_s, q_r, c_s, c_r, g_s, g_r,
+    step_on, isem, hsem, ag_s, ag_r, y_s, y_r, z_s, z_r, b_s, b_r, l_s, l_r, r_s, r_r, q_s, q_r, c_s, c_r, g_s, g_r,
 ):
     S = 4 * per
     mp, f = lax.axis_index("mp"), lax.axis_index("fsdp")
@@ -55,7 +55,7 @@
         lax.fori_loop(0, n, step, 0)
 
     def chunk(ci):
-        return lax.rem((ci + 1) // 2, 2), ci // 2
+        return lax.rem((ci + 1) // 2, 2), lax.rem(core + ci // 2, 2)
 
     def ydev(d):
         return lax.rem(y + d, 4)
@@ -76,17 +76,12 @@
     def greet(dev):
         pl.semaphore_signal(bar, inc=1, device_id=dev, device_id_type=MESH)
 
-    loop(15, lambda i: greet({"fsdp": lax.rem(f + i + 1, 16)}))
+    loop(3, lambda i: greet({"fsdp": h * 8 + lax.rem(x + i + 1, 4) * 2 + core}))
+    greet(sibling)
     loop(3, lambda i: greet(mate(i + 1)))
-
-    @pl.when(edge)
-    def _():
-        greet({"mp": y * 4 + zin})
-
-    @pl.when(inner)
-    def _():
-        greet({"mp": y * 4 + zout})
-        greet({"mp": y * 4 + 3 - z})
+    up = {"mp": y * 4 + lax.rem(z + 1, 4), "fsdp": jnp.where(z == 3, lax.rem(f + 8, 16), f)}
+    greet(up)
+    greet({"mp": y * 4 + lax.rem(z + 3, 4), "fsdp": jnp.where(z == 0, lax.rem(f + 8, 16), f)})
 
     for hh in range(2):
         r = jnp.int32(0)
@@ -129,13 +124,7 @@
     lax.fori_loop(0, ROWS, pool, 0, unroll=4)
     pb[core, x] = (ns[...] * gain[...] * 0.25).astype(jnp.bfloat16)
 
-    @pl.when(edge)
-    def _():
-        pl.semaphore_wait(bar, 19)
-
-    @pl.when(inner)
-    def _():
-        pl.semaphore_wait(bar, 20)
+    pl.semaphore_wait(bar, 9)
 
     def spread(c, i):
         for k, dx in enumerate((1, 3, 2)):
@@ -148,7 +137,10 @@
             arrived(pb.at[c, xx], ag_r.at[c, xx])
             start(pb.at[c, xx], pb.at[c, xx], ag_s.at[i + k], ag_r.at[c, xx], sibling)
 
-    start(pb.at[core, x], pb.at[2 + core, x], ag_s.at[0], ag_r.at[2 + core, x], other)
+    def tell(i):
+        pl.semaphore_signal(step_on.at[i], inc=1, device_id=up, device_id_type=MESH)
+
+    tell(0)
     spread(core, 1)
 
     ct[...] = codes[...].T
@@ -169,11 +161,16 @@
 
         loop(8, part)
 
-        @pl.when(lc == 0)
-        def _():
-            hand_on(core, 5)
-
-    loop(per, turn)
+    for i in range(3):
+        if i < per:
+            turn(i)
+        pl.semaphore_wait(step_on.at[i], 1)
+        if i < 2:
+            tell(i + 1)
+    start(pb.at[core, x], pb.at[2 + core, x], ag_s.at[0], ag_r.at[2 + core, x], other)
+    for i in range(3, per):
+        turn(i)
+    hand_on(core, 5)
 
     def stage_m1(s):
         ci = s // per
@@ -181,7 +178,7 @@
         rel, cc = chunk(ci)
         c = rel * 2 + cc
 
-        @pl.when(jnp.logical_and(lc == 0, core != cc))
+        @pl.when(jnp.logical_and(lc == 0, ci >= 2))
         def _():
             loop(4, lambda i: arrived(pb.at[c, i], ag_r.at[c, i]))
 
@@ -319,15 +316,14 @@
                 start(lr.at[ci, xx], lrr.at[rel, me], q_s.at[ci, dx], q_r.at[rel, me], dev)
 
             loop(3, lambda i: give(i + 1))
-            pl.when(core != cc)(lambda: give(0))
+            pl.when(ci >= 2)(lambda: give(0))
             loop(3, lambda i: arrived(lr.at[ci, ydev(i + 1)], l_r.at[ci, ydev(i + 1)]))
             loop(3, lambda i: give_loss(i + 1))
-            pl.when(core != cc)(lambda: give_loss(0))
+            pl.when(ci >= 2)(lambda: give_loss(0))
 
     def gather_sum(rel):
-        ci = jnp.where(core == 0, rel, 3 - rel)
         out_acc[...] = dp[rel * 2 + core, x]
-        accl[...] = lr[ci, x]
+        accl[...] = lr[rel, x]
 
         def add(i):
             src = lax.rem(me + 1 + i, 8)
@@ -342,16 +338,16 @@
         pl.when(jnp.logical_and(t >= lag, t < S + lag))(lambda: fn(t - lag))
 
     def tick(t):
+        @pl.when(t == per)
+        def _():
+            hand_on(2 + core, 12)
+
         pl.when(t < S)(lambda: stage_m1(t))
 
-        @pl.when(t == 0)
+        @pl.when(t == per - 1)
         def _():
             arrived(pb.at[2 + core, x], ag_r.at[2 + core, x])
             spread(2 + core, 8)
-
-        @pl.when(t == per - 1)
-        def _():
-            hand_on(2 + core, 12)
 
         stage(t, EDGE, stage_edge)
         stage(t, CROSS, stage_cross)
@@ -407,7 +403,7 @@
         for d in (1, 2, 3):
             sent(ls.at[ci, 0], l_s.at[ci, d])
             both(d)
-        pl.when(core != ci // 2)(lambda: both(0))
+        pl.when(ci >= 2)(lambda: both(0))
 
     loop(4, chunk_left)
 
@@ -433,7 +429,7 @@
         pltpu.SMEM((16,), jnp.int32), pltpu.SMEM((8 + K,), jnp.int32),
     ]
     scratch += [
-        dma, dma((per,)), dma((15,)), dma((4, 4)), dma((S, 4)), dma((S, 4)), dma((S, 2)), dma((S, 2)),
+        pltpu.SemaphoreType.REGULAR((3,)), dma, dma((per,)), dma((15,)), dma((4, 4)), dma((S, 4)), dma((S, 4)), dma((S, 2)), dma((S, 2)),
         dma((S, 4)), dma((S, 4)), dma((4, 4)), dma((4, 4)), dma((4, 4)), dma((2, 8)), dma((4, 4)), dma((2, 8)),
         dma((2,)), dma((2,)), dma((16,)), dma((16,)),
     ]

time: 85.4 us -> 84 us (0.984)
  Pallas kernels: 82.6 us -> 80.6 us
    pallas_call x1, Pallas kernels: 80 us -> 78 us  [call(): pl.pallas_call(functools.partial(kernel, K, per), name='distill%d' % K, o...]
where the time goes in v3:
time: 84 us; the launch traced here: 83.8 us
  Pallas kernels  80.6 us (96%)
  between operations  1.94 us (2%)
  other arithmetic  1.3 us (2%)
    pallas_call x1, Pallas kernels, call(): pl.pallas_call(functools.partial(kernel, K, per), name='distill%d' % K, o...  78 us
    pallas_call x1, Pallas kernels, last(): pl.pallas_call(finish, name='finish', grid=(2,), out_shape=(jax.ShapeDtyp...  2.59 us

profile of v3, /device:TPU:1, one launch (start us, length us, event | category | flops | bytes accessed | tf_op | source)
XLA Modules:
  0.0 83.8 jit_solution(2547030375773965712)
XLA Ops:
  0.6 1.3 %fusion = s32[]{:T(128)} fusion(s32[16]{0:T(128)} %param.11), kind=kLoop, calls=%fused_computation.1 | loop fusion | flops 111 | bytes 68 | tf_op jit(solution)/shard_map/reduce_sum | solution.py:501
  3.2 78.0 %conditional.1 = ((f32[16,2048]{1,0:T(8,128)S(1)}, f32[8,128]{1,0:T(8,128)S(1)}, f32[1,2048]{1,0:T(1,128)S(1)}, f32[16,16,128]{2,1,0:T(8,128)S(1)})) conditional(s32[]{:T(128)} %clamp.3, (s32[16]{0:T(128)}, f32[1,2048]{1,0:T(1,128)}, s32[16,256]{1,0:T(8,128)}, bf16[1,16,16,2048]{3,2,1,0:T(8,128)(2,1)}, ...), branch_computations={%region_1.0_spmd, %region_2.0_spmd, %region_3.0_spmd} | conditional | bytes 8 | solution.py:505
  3.2 78.0 %distill4.1 = (f32[16,2048]{1,0:T(8,128)S(1)}, f32[8,128]{1,0:T(8,128)S(1)}, f32[1,2048]{1,0:T(1,128)S(1)}, f32[16,16,128]{2,1,0:T(8,128)S(1)}) custom-call(s32[16]{0:T(128)} %get-tuple-element.30.partner, f32[1,2048]{1,0:T(1,128)} %get-tuple-element.31.gain, s32[16,256]{1,0:T(8,128)} %get-tuple-element.32.codes, ...), custom_call_target="tpu_custom_call" | custom-call | tf_op jit(solution)/shard_map/cond/branch_0_fun/distill4/pallas_call | solution.py:437
  81.2 2.6 %finish.1 = (bf16[1,16,16,2048]{3,2,1,0:T(8,128)(2,1)}, f32[1,16]{1,0:T(1,128)}, f32[1,2048]{1,0:T(1,128)}) custom-call(f32[16,2048]{1,0:T(8,128)S(1)} %get-tuple-element.52.acc, f32[1,2048]{1,0:T(1,128)} %gain.1, f32[16,16,128]{2,1,0:T(8,128)S(1)} %get-tuple-element.53.inv, f32[8,128]{1,0:T(8,128)S(1)} %get-tuple-element.54.loss, ...), custom_call_target="tpu_custom_call" | custom-call | tf_op jit(solution)/shard_map/finish/pallas_call | solution.py:481

commit v4 on v3

--- a/solution.py
+++ b/solution.py
@@ -13,7 +13,8 @@
 LC = 768
 ROWS = 16
 SIZES = (4, 6, 8)
-EDGE, CROSS, BACK, EW, M2 = 2, 4, 6, 9, 11
+EDGE, CROSS, BACK, EW, M2 = 2, 4, 6, 8, 10
+EARLY, GAP = 1, 0
 
 
 def kernel(
@@ -57,6 +58,15 @@
     def chunk(ci):
         return lax.rem((ci + 1) // 2, 2), lax.rem(core + ci // 2, 2)
 
+    first = per + EARLY
+
+    def work(s):
+        late = s - EARLY
+        mid = jnp.logical_and(s >= first, late < 3 * per)
+        ci = jnp.where(s < per, 0, jnp.where(mid, late // per, 3))
+        lc = jnp.where(s < per, s, jnp.where(s < first, s - per, jnp.where(mid, lax.rem(late, per), s - 3 * per)))
+        return ci, lc
+
     def ydev(d):
         return lax.rem(y + d, 4)
 
@@ -173,8 +183,7 @@
     hand_on(core, 5)
 
     def stage_m1(s):
-        ci = s // per
-        lc = s - ci * per
+        ci, lc = work(s)
         rel, cc = chunk(ci)
         c = rel * 2 + cc
 
@@ -228,8 +237,7 @@
             start(es.at[s], outer(s), z_s.at[s, 0], z_r.at[s, 0], {"mp": y * 4 + zout})
 
     def stage_ew(s):
-        ci = s // per
-        lc = s - ci * per
+        ci, lc = work(s)
         rel, cc = chunk(ci)
 
         @pl.when(edge)
@@ -255,7 +263,8 @@
             rr = 1.0 / (a1 * b1)
             pos = v >= 0.0
             s12 = (jnp.where(pos, 1.0, e2) * a1 + jnp.where(pos, 1.0, e) * b1) * rr
-            t = 1.0 / (1.0 + jnp.exp(q * -0.5))
+            eq = jnp.exp(jnp.abs(q) * -0.5)
+            t = jnp.where(q >= 0.0, 1.0, eq) / (1.0 + eq)
             db[s, j] = (s12 - target - t).astype(jnp.bfloat16)
             each = 2.0 * jnp.maximum(v, 0.0) + jnp.log(a1 * a1 * b1) - (t + target) * v
             part = each[:, 0:128]
@@ -287,8 +296,7 @@
         return xx, {"fsdp": h * 8 + xx * 2 + cc}
 
     def stage_m2(s):
-        ci = s // per
-        lc = s - ci * per
+        ci, lc = work(s)
         rel, cc = chunk(ci)
         c = rel * 2 + cc
         loop(3, lambda i: arrived(dl.at[s, ydev(i + 1)], b_r.at[s, ydev(i + 1)]))
@@ -335,37 +343,38 @@
         loop(7, add)
 
     def stage(t, lag, fn):
-        pl.when(jnp.logical_and(t >= lag, t < S + lag))(lambda: fn(t - lag))
+        u = t - lag
+        late = u >= first + GAP
+        on = jnp.logical_and(u >= 0, jnp.logical_or(u < first, late))
+        s = jnp.where(late, u - GAP, u)
+        pl.when(jnp.logical_and(on, s < S))(lambda: fn(s))
 
     def tick(t):
-        @pl.when(t == per)
+        @pl.when(t == first + GAP)
         def _():
             hand_on(2 + core, 12)
 
-        pl.when(t < S)(lambda: stage_m1(t))
-
-        @pl.when(t == per - 1)
+        stage(t, 0, stage_m1)
+        stage(t, EDGE, stage_edge)
+        stage(t, CROSS, stage_cross)
+
+        @pl.when(t == first + max(GAP - 3, -1))
         def _():
             arrived(pb.at[2 + core, x], ag_r.at[2 + core, x])
             spread(2 + core, 8)
 
-        stage(t, EDGE, stage_edge)
-        stage(t, CROSS, stage_cross)
         stage(t, BACK, stage_back)
         stage(t, EW, stage_ew)
         stage(t, M2, stage_m2)
 
-        @pl.when(t == S - 2 + M2)
-        def _():
-            gather_sum(1)
-            cb[...] = out_acc[...].astype(jnp.bfloat16)
-            clb[...] = accl[...]
-            start(cb, cr, c_s.at[0], c_r.at[0], other)
-            start(clb, clr, c_s.at[1], c_r.at[1], other)
-
-    loop(S + M2, tick)
+    loop(S + GAP + M2, tick)
 
     loop(15, lambda i: start(gg.at[f], gg.at[f], g_s.at[i + 1], g_r.at[f], {"fsdp": lax.rem(f + 1 + i, 16)}))
+    gather_sum(1)
+    cb[...] = out_acc[...].astype(jnp.bfloat16)
+    clb[...] = accl[...]
+    start(cb, cr, c_s.at[0], c_r.at[0], other)
+    start(clb, clr, c_s.at[1], c_r.at[1], other)
     gather_sum(0)
     arrived(cr, c_r.at[0])
     arrived(clr, c_r.at[1])
@@ -500,9 +509,12 @@
     away = ((ids & 3) < 2) & ((partner & 3) >= 2)
     crossing = jnp.sum(away.astype(jnp.int32))
     args = (hidden, gain, head, partner, codes.T)
-    calls = [functools.partial(call, K, i + 1) for i, K in enumerate(SIZES)]
-    which = sum((crossing > K).astype(jnp.int32) for K in SIZES[:-1])
-    acc, loss, total, inv = lax.switch(which, calls, *args) if len(SIZES) > 1 else calls[0](*args)
+    k0, k1, k2 = [functools.partial(call, K, i + 1) for i, K in enumerate(SIZES)]
+
+    def more(*args):
+        return lax.cond(crossing > SIZES[1], k2, k1, *args)
+
+    acc, loss, total, inv = lax.cond(crossing > SIZES[0], more, k0, *args)
     return last(acc, gain, inv, loss, total, hidden)
 
 

time: 84 us -> 83.9 us (level)
  no operation moved by 1% of the time
where the time goes in v4:
time: 83.9 us; the launch traced here: 83.7 us
  Pallas kernels  81.1 us (97%)
  other arithmetic  1.3 us (2%)
  between operations  1.29 us (2%)
    pallas_call x1, Pallas kernels, call(): pl.pallas_call(functools.partial(kernel, K, per), name='distill%d' % K, o...  78.4 us
    pallas_call x1, Pallas kernels, last(): pl.pallas_call(finish, name='finish', grid=(2,), out_shape=(jax.ShapeDtyp...  2.68 us

profile of v4, /device:TPU:1, one launch (start us, length us, event | category | flops | bytes accessed | tf_op | source)
XLA Modules:
  0.0 83.7 jit_solution(16416255964238959928)
XLA Ops:
  0.6 1.3 %fusion = s32[]{:T(128)} fusion(s32[16]{0:T(128)} %param.12), kind=kLoop, calls=%fused_computation.1 | loop fusion | flops 111 | bytes 68 | tf_op jit(solution)/shard_map/reduce_sum | solution.py:510
  2.6 78.5 %conditional.2 = ((f32[16,2048]{1,0:T(8,128)}, f32[8,128]{1,0:T(8,128)}, f32[1,2048]{1,0:T(1,128)}, f32[16,16,128]{2,1,0:T(8,128)})) conditional(s32[]{:T(128)} %convert_element_type.10, (s32[16]{0:T(128)}, f32[1,2048]{1,0:T(1,128)}, s32[16,256]{1,0:T(8,128)}, bf16[1,16,16,2048]{3,2,1,0:T(8,128)(2,1)}, bf16[1,2048,2304]{2,1,0:T(8,128)(2,1)}) %tuple.29, ...), branch_computations={%region_1.0_spmd, %region_2.0_spmd} | conditional | flops 2 | bytes 62 | solution.py:517
  2.6 78.4 %distill4.1 = (f32[16,2048]{1,0:T(8,128)}, f32[8,128]{1,0:T(8,128)}, f32[1,2048]{1,0:T(1,128)}, f32[16,16,128]{2,1,0:T(8,128)}) custom-call(s32[16]{0:T(128)} %get-tuple-element.42.partner, f32[1,2048]{1,0:T(1,128)} %get-tuple-element.43.gain, s32[16,256]{1,0:T(8,128)} %get-tuple-element.44.codes, bf16[1,16,16,2048]{3,2,1,0:T(8,128)(2,1)} %get-tuple-element.45.hidden, ...), custom_call_target="tpu_custom_call" | custom-call | tf_op jit(solution)/shard_map/cond/branch_0_fun/distill4/pallas_call | solution.py:446
  81.0 2.7 %finish.1 = (bf16[1,16,16,2048]{3,2,1,0:T(8,128)(2,1)}, f32[1,16]{1,0:T(1,128)}, f32[1,2048]{1,0:T(1,128)}) custom-call(f32[16,2048]{1,0:T(8,128)} %get-tuple-element.70.acc, f32[1,2048]{1,0:T(1,128)} %gain.1, f32[16,16,128]{2,1,0:T(8,128)} %get-tuple-element.71.inv, f32[8,128]{1,0:T(8,128)} %get-tuple-element.72.loss, f32[1,2048]{1,0:T(1,128)} %get-tuple-element.73.total, ...), custom_call_target="tpu_custom_call" | custom-call | tf_op jit(solution)/shard_map/finish/pallas_call | solution.py:490
